TPU v7x, 32 devices: a whole 2x2x4 slice. The times are simulated.
32 devices in a mesh: seq: 16 (over z, x, core), rows: 2 (over y).
Axes of the slice: x: 2, y: 2, z: 4, core: 2. Of those that a mesh axis runs over, the one named last changes fastest.
Arguments:
- tokens: bfloat16 [2048, 4, 512], P('seq', 'rows'), may hold values from -6 to 6
- memory: bfloat16 [1024, 4, 512], P('seq', 'rows'), may hold values from -6 to 6
- segments: int32 [4, 2048], P('rows', 'seq'), may hold values from 0 to 1023, as said below
- padding: int32 [4, 2048], P('rows', 'seq'), may hold values from 0 to 1, as said below
- cotangent: bfloat16 [2048, 4, 512], P('seq', 'rows'), may hold values from -6 to 6
- self_project: bfloat16 [512, 1536], replicated, may hold values from -0.25 to 0.25
- self_output: bfloat16 [512, 512], replicated, may hold values from -1 to 1
- cross_query: bfloat16 [512, 512], replicated, may hold values from -0.25 to 0.25
- cross_memory: bfloat16 [512, 1024], replicated, may hold values from -0.25 to 0.25
- cross_output: bfloat16 [512, 512], replicated, may hold values from -1 to 1
- feed_in: bfloat16 [512, 2048], replicated, may hold values from -0.25 to 0.25
- feed_in_bias: float32 [2048], replicated, may hold values from -3 to 3
- feed_out: bfloat16 [2048, 512], replicated, may hold values from -0.125 to 0.125
- feed_out_bias: float32 [512], replicated, may hold values from -3 to 3
- norm_gain: float32 [3, 512], replicated, may hold values from 0.25 to 1.75
- norm_bias: float32 [3, 512], replicated, may hold values from -3 to 3
- residual_scale: float32 [3, 512], replicated, may hold values from 0.6 to 2.5
Outputs:
- output: bfloat16 [2048, 4, 512], P('seq', 'rows')
- tokens_grad: float32 [2048, 4, 512], P('seq', 'rows')
- memory_grad: float32 [1024, 4, 512], P('seq', 'rows')
- self_project_grad: float32 [512, 1536], P('seq')
- self_output_grad: float32 [512, 512], P('seq')
- cross_query_grad: float32 [512, 512], P('seq')
- cross_memory_grad: float32 [512, 1024], P('seq')
- cross_output_grad: float32 [512, 512], P('seq')
- feed_in_grad: float32 [512, 2048], P('seq')
- feed_in_bias_grad: float32 [2048], P('seq')
- feed_out_grad: float32 [2048, 512], P('seq')
- feed_out_bias_grad: float32 [512], P('seq')
- norm_gain_grad: float32 [3, 512], P(None, 'seq')
- norm_bias_grad: float32 [3, 512], P(None, 'seq')
- residual_scale_grad: float32 [3, 512], P(None, 'seq')
Inputs may be any that keep to these rules, and one draw needn't show every extreme that they name: `segments`: rows come in aligned pairs. In each pair one row, which one drawn from the seed, is a document row: segment 0 at every position. The other is packed: its ids never fall, change only at even positions, each id covers 2 to 62 positions (the last one possibly fewer, at least 2), and the id of its last segment is exactly 1023. `padding`: 1 on every position of document rows. On a packed row it is 0 exactly on the positions of its last segment, in some packed rows, and 1 elsewhere.
All inputs are finite; a program needn't handle non-finite values.
Results may differ from a plain program's by a relative error of at most 0.025.
Values may be sent and summed in bfloat16 or wider, within the bound.
A program may use at most 256 MiB of HBM per device.

v0:
```python
import math

import jax
import jax.numpy as jnp
from jax import lax
from jax.sharding import PartitionSpec as P

HEADS = 8


EPSILON = 1e-05
NEGATIVE = -1e30
score_block = 512


def norm_forward(summed, gain_row, shift_row):
    centre = jnp.mean(summed, -1, keepdims=True)
    centred = summed - centre
    inverse_std = lax.rsqrt(jnp.mean(centred * centred, -1, keepdims=True) + EPSILON)
    normed = centred * inverse_std
    return (normed * gain_row + shift_row, normed, inverse_std)


def norm_backward(gradient, normed, inverse_std, gain_row):
    scaled = gradient * gain_row
    centred = (
        scaled
        - jnp.mean(scaled, -1, keepdims=True)
        - normed * jnp.mean(scaled * normed, -1, keepdims=True)
    )
    return (centred * inverse_std, jnp.sum(gradient * normed, 0), jnp.sum(gradient, 0))


def split_heads(packed, head_count):
    return packed.reshape(packed.shape[:2] + (head_count, packed.shape[2] // head_count))


def to_heads(packed, head_count):
    return split_heads(packed, head_count).transpose(1, 2, 0, 3)


def from_heads(head_grid):
    row_count, head_count, extent, head_width = head_grid.shape
    return head_grid.transpose(2, 0, 1, 3).reshape(extent * row_count, head_count * head_width)


def by_rows(row_fn, row_first, key_second, out_dims):
    moved = tuple((jnp.moveaxis(array, 1, 0) for array in key_second))

    def one_row(element):
        firsts, seconds = element
        outcome = row_fn(
            tuple((array[None] for array in firsts)), tuple((array[:, None] for array in seconds))
        )
        return tuple((array.squeeze(dim) for array, dim in zip(outcome, out_dims)))

    outcome = lax.map(one_row, (row_first, moved))
    return tuple((jnp.moveaxis(array, 0, dim) for array, dim in zip(outcome, out_dims)))


def self_mask(query_segs, query_places, key_segs, key_pads, key_places):
    same_segment = query_segs[:, :, None] == key_segs[:, None, :]
    causal = key_places[None, None, :] <= query_places[None, :, None]
    itself = key_places[None, None, :] == query_places[None, :, None]
    return same_segment & causal & ((key_pads[:, None, :] == 1) | itself)


def cross_mask(query_segs, key_segs):
    return query_segs[:, :, None] == key_segs[:, None, :]


def scores_of(queries, key_heads, allowed):
    score_scale = 1.0 / math.sqrt(queries.shape[-1])
    raw_scores = (
        jnp.einsum("rhqd,krhd->rhqk", queries, key_heads, preferred_element_type=jnp.float32)
        * score_scale
    )
    return jnp.where(allowed[:, None], raw_scores, NEGATIVE)


def forward_update(carried, queries, key_heads, value_heads, allowed):

    def row_step(firsts, seconds):
        running_max, normalizer, weighted, query_row, allowed_row = firsts
        key_row, value_row = seconds

        def run(current):
            old_max, old_total, old_weighted = current
            scores = scores_of(query_row, key_row, allowed_row)
            new_max = jnp.maximum(old_max, jnp.max(scores, -1))
            weights = jnp.where(allowed_row[:, None], jnp.exp(scores - new_max[..., None]), 0.0)
            decay_factor = jnp.exp(old_max - new_max)
            new_total = old_total * decay_factor + jnp.sum(weights, -1)
            new_weighted = old_weighted * decay_factor[..., None] + jnp.einsum(
                "rhqk,krhd->rhqd",
                weights.astype(jnp.bfloat16),
                value_row,
                preferred_element_type=jnp.float32,
            )
            return (new_max, new_total, new_weighted)

        return lax.cond(
            jnp.any(allowed_row), run, lambda current: current, (running_max, normalizer, weighted)
        )

    return by_rows(
        row_step, tuple(carried) + (queries, allowed), (key_heads, value_heads), (0, 0, 0)
    )


def grad_parts(queries, key_heads, value_heads, grad_heads, log_totals, deltas, allowed):
    scores = scores_of(queries, key_heads, allowed)
    weights = jnp.where(allowed[:, None], jnp.exp(scores - log_totals[..., None]), 0.0)
    grad_weights = jnp.einsum(
        "rhqd,krhd->rhqk", grad_heads, value_heads, preferred_element_type=jnp.float32
    )
    grad_scores = (weights * (grad_weights - deltas[..., None])).astype(jnp.bfloat16)
    return (weights.astype(jnp.bfloat16), grad_scores)


def query_grad(queries, key_heads, value_heads, grad_heads, log_totals, deltas, allowed):
    score_scale = 1.0 / math.sqrt(queries.shape[-1])
    weights, grad_scores = grad_parts(
        queries, key_heads, value_heads, grad_heads, log_totals, deltas, allowed
    )
    return (
        jnp.einsum("rhqk,krhd->rhqd", grad_scores, key_heads, preferred_element_type=jnp.float32)
        * score_scale
    )


def key_grads(queries, key_heads, value_heads, grad_heads, log_totals, deltas, allowed):
    score_scale = 1.0 / math.sqrt(queries.shape[-1])
    weights, grad_scores = grad_parts(
        queries, key_heads, value_heads, grad_heads, log_totals, deltas, allowed
    )
    grad_keys = (
        jnp.einsum("rhqk,rhqd->krhd", grad_scores, queries, preferred_element_type=jnp.float32)
        * score_scale
    )
    grad_values = jnp.einsum(
        "rhqk,rhqd->krhd", weights, grad_heads, preferred_element_type=jnp.float32
    )
    return (grad_keys, grad_values)


def block_scan(carried, arrays, offset, block_step):
    extent_all = arrays[0].shape[0]
    extent = math.gcd(extent_all, score_block)
    blocks = extent_all // extent
    stacked = tuple((array.reshape((blocks, extent) + array.shape[1:]) for array in arrays))

    def inner_step(current, element):
        number, portion = element
        return (block_step(current, portion, offset + number * extent), None)

    carried, unused = lax.scan(inner_step, carried, (jnp.arange(blocks, dtype=jnp.int32), stacked))
    return carried


def block_map(arrays, block_step):
    extent_all = arrays[0].shape[0]
    extent = math.gcd(extent_all, score_block)
    blocks = extent_all // extent
    stacked = tuple((array.reshape((blocks, extent) + array.shape[1:]) for array in arrays))

    def inner_step(element):
        number, portion = element
        return block_step(portion, number * extent)

    outcome = lax.map(inner_step, (jnp.arange(blocks, dtype=jnp.int32), stacked))
    return outcome.reshape((extent_all,) + outcome.shape[2:])


def forward_folder(queries, mask_of, model_width, head_count):

    def block_step(carried, portion, offset):
        allowed = mask_of(portion, offset)
        block_keys = portion[0]
        return forward_update(
            carried,
            queries,
            split_heads(block_keys[..., :model_width], head_count),
            split_heads(block_keys[..., model_width:], head_count),
            allowed,
        )

    def folder(carried, portion, offset):
        return block_scan(carried, portion, offset, block_step)

    return folder


def query_stepper(queries, grad_heads, log_totals, deltas, mask_of, model_width, head_count):

    def block_step(carried, portion, offset):
        allowed = mask_of(portion, offset)
        block_keys = portion[0]

        def row_step(firsts, seconds):
            current, query_row, grad_row, total_row, delta_row, allowed_row = firsts
            key_row, value_row = seconds

            def run(value):
                return value + query_grad(
                    query_row, key_row, value_row, grad_row, total_row, delta_row, allowed_row
                )

            return (lax.cond(jnp.any(allowed_row), run, lambda value: value, current),)

        return by_rows(
            row_step,
            (carried, queries, grad_heads, log_totals, deltas, allowed),
            (
                split_heads(block_keys[..., :model_width], head_count),
                split_heads(block_keys[..., model_width:], head_count),
            ),
            (0,),
        )[0]

    return block_step


def key_stepper(queries, grad_heads, log_totals, deltas, mask_of, model_width, head_count):

    def block_step(portion, offset):
        allowed = mask_of(portion, offset)
        block_keys = portion[0]
        extent = block_keys.shape[0]

        def row_step(firsts, seconds):
            query_row, grad_row, total_row, delta_row, allowed_row = firsts
            key_row, value_row = seconds

            def run(unused):
                grad_keys, grad_values = key_grads(
                    query_row, key_row, value_row, grad_row, total_row, delta_row, allowed_row
                )
                return jnp.concatenate(
                    [
                        grad_keys.reshape(extent, 1, model_width),
                        grad_values.reshape(extent, 1, model_width),
                    ],
                    -1,
                )

            def skip(unused):
                return jnp.zeros((extent, 1, 2 * model_width), jnp.float32)

            return (lax.cond(jnp.any(allowed_row), run, skip, 0),)

        return by_rows(
            row_step,
            (queries, grad_heads, log_totals, deltas, allowed),
            (
                split_heads(block_keys[..., :model_width], head_count),
                split_heads(block_keys[..., model_width:], head_count),
            ),
            (1,),
        )[0]

    return block_step


def on_device(
    tokens,
    memory,
    segments,
    padding,
    cotangent,
    self_project,
    self_output,
    cross_query,
    cross_memory,
    cross_output,
    feed_in,
    feed_in_bias,
    feed_out,
    feed_out_bias,
    norm_gain,
    norm_bias,
    residual_scale,
):
    seq_len, row_count, model_width = tokens.shape
    mem_len = memory.shape[0]
    head_count = HEADS
    head_width = model_width // head_count
    token_count = seq_len * row_count
    places = lax.axis_index("seq") * seq_len + jnp.arange(seq_len, dtype=jnp.int32)
    seg_columns = segments.T
    pad_columns = padding.T
    memory_segments = segments[:, ::2]
    memory_columns = memory_segments.T

    def self_key_mask(portion, offset):
        extent = portion[0].shape[0]
        return self_mask(
            segments,
            places,
            portion[1].T,
            portion[2].T,
            offset + jnp.arange(extent, dtype=jnp.int32),
        )

    def cross_key_mask(portion, offset):
        return cross_mask(segments, portion[1].T)

    def empty_state():
        return (
            jnp.full((row_count, head_count, seq_len), NEGATIVE, jnp.float32),
            jnp.zeros((row_count, head_count, seq_len), jnp.float32),
            jnp.zeros((row_count, head_count, seq_len, head_width), jnp.float32),
        )

    flattened = tokens.reshape(token_count, model_width)
    xfloat = flattened.astype(jnp.float32)
    projected = jnp.dot(flattened, self_project, preferred_element_type=jnp.float32).astype(
        jnp.bfloat16
    )
    query_flat = projected[:, :model_width].reshape(seq_len, row_count, model_width)
    queries = to_heads(query_flat, head_count)
    key_values = projected[:, model_width:].reshape(seq_len, row_count, 2 * model_width)
    self_fold = forward_folder(queries, self_key_mask, model_width, head_count)
    self_max, self_total, self_weighted = self_fold(
        empty_state(),
        (
            lax.all_gather(key_values, "seq", axis=0, tiled=True),
            lax.all_gather(seg_columns, "seq", axis=0, tiled=True),
            lax.all_gather(pad_columns, "seq", axis=0, tiled=True),
        ),
        jnp.int32(0),
    )
    self_heads = self_weighted / self_total[..., None]
    self_lse = self_max + jnp.log(self_total)
    self_attended = from_heads(self_heads).astype(jnp.bfloat16)
    first_branch = jnp.dot(self_attended, self_output, preferred_element_type=jnp.float32)
    hidden1, normed1, inverse1 = norm_forward(
        xfloat * residual_scale[0] + first_branch, norm_gain[0], norm_bias[0]
    )
    hidden1_low = hidden1.astype(jnp.bfloat16)
    cross_flat = jnp.dot(hidden1_low, cross_query, preferred_element_type=jnp.float32).astype(
        jnp.bfloat16
    )
    cross_query_block = cross_flat.reshape(seq_len, row_count, model_width)
    cross_queries = to_heads(cross_query_block, head_count)
    memory_flat = memory.reshape(mem_len * row_count, model_width)
    memory_key_values = (
        jnp.dot(memory_flat, cross_memory, preferred_element_type=jnp.float32)
        .astype(jnp.bfloat16)
        .reshape(mem_len, row_count, 2 * model_width)
    )
    cross_fold = forward_folder(cross_queries, cross_key_mask, model_width, head_count)
    cross_max, cross_total, cross_weighted = cross_fold(
        empty_state(),
        (
            lax.all_gather(memory_key_values, "seq", axis=0, tiled=True),
            lax.all_gather(memory_columns, "seq", axis=0, tiled=True),
        ),
        jnp.int32(0),
    )
    cross_heads = cross_weighted / cross_total[..., None]
    cross_lse = cross_max + jnp.log(cross_total)
    cross_attended = from_heads(cross_heads).astype(jnp.bfloat16)
    second_branch = jnp.dot(cross_attended, cross_output, preferred_element_type=jnp.float32)
    hidden2, normed2, inverse2 = norm_forward(
        hidden1 * residual_scale[1] + second_branch, norm_gain[1], norm_bias[1]
    )
    hidden2_low = hidden2.astype(jnp.bfloat16)
    pre_active = jnp.dot(hidden2_low, feed_in, preferred_element_type=jnp.float32) + feed_in_bias
    active_value, gelu_back = jax.vjp(jax.nn.gelu, pre_active)
    active = active_value.astype(jnp.bfloat16)
    third_branch = jnp.dot(active, feed_out, preferred_element_type=jnp.float32) + feed_out_bias
    result, normed3, inverse3 = norm_forward(
        hidden2 * residual_scale[2] + third_branch, norm_gain[2], norm_bias[2]
    )
    output = result.astype(jnp.bfloat16).reshape(seq_len, row_count, model_width)
    gradient = cotangent.reshape(token_count, model_width).astype(jnp.float32)
    grad_total3, gain_third, shift_third = norm_backward(gradient, normed3, inverse3, norm_gain[2])
    scale_third = jnp.sum(grad_total3 * hidden2, 0)
    grad_third = grad_total3.astype(jnp.bfloat16)
    grad_feed_out = jnp.dot(active.T, grad_third, preferred_element_type=jnp.float32)
    grad_feed_out_bias = jnp.sum(grad_third.astype(jnp.float32), 0)
    grad_active = jnp.dot(grad_third, feed_out.T, preferred_element_type=jnp.float32)
    grad_pre = gelu_back(grad_active)[0].astype(jnp.bfloat16)
    grad_feed_in = jnp.dot(hidden2_low.T, grad_pre, preferred_element_type=jnp.float32)
    grad_feed_in_bias = jnp.sum(grad_pre.astype(jnp.float32), 0)
    grad_hidden2 = grad_total3 * residual_scale[2] + jnp.dot(
        grad_pre, feed_in.T, preferred_element_type=jnp.float32
    )
    grad_total2, gain_second, shift_second = norm_backward(
        grad_hidden2, normed2, inverse2, norm_gain[1]
    )
    scale_second = jnp.sum(grad_total2 * hidden1, 0)
    grad_second = grad_total2.astype(jnp.bfloat16)
    grad_cross_output = jnp.dot(cross_attended.T, grad_second, preferred_element_type=jnp.float32)
    grad_cross = jnp.dot(grad_second, cross_output.T, preferred_element_type=jnp.float32).astype(
        jnp.bfloat16
    )
    grad_cross_block = grad_cross.reshape(seq_len, row_count, model_width)
    grad_cross_heads = to_heads(grad_cross_block, head_count)
    cross_delta = jnp.sum(grad_cross_heads.astype(jnp.float32) * cross_heads, -1)
    zero_grid = jnp.zeros((row_count, head_count, seq_len, head_width), jnp.float32)
    cross_query_step = query_stepper(
        cross_queries,
        grad_cross_heads,
        cross_lse,
        cross_delta,
        cross_key_mask,
        model_width,
        head_count,
    )
    whole_memory, whole_memory_segs = (
        lax.all_gather(memory_key_values, "seq", axis=0, tiled=True),
        lax.all_gather(memory_columns, "seq", axis=0, tiled=True),
    )
    grad_cross_queries = block_scan(
        zero_grid, (whole_memory, whole_memory_segs), 0, cross_query_step
    )
    cross_key_step = key_stepper(
        cross_queries,
        grad_cross_heads,
        cross_lse,
        cross_delta,
        cross_key_mask,
        model_width,
        head_count,
    )
    portion = (whole_memory, whole_memory_segs)
    grad_memory_kv = lax.psum_scatter(
        block_map(portion, cross_key_step).astype(jnp.bfloat16),
        "seq",
        scatter_dimension=0,
        tiled=True,
    ).astype(jnp.float32)
    grad_cross_flat = from_heads(grad_cross_queries).astype(jnp.bfloat16)
    grad_memory_low = grad_memory_kv.reshape(mem_len * row_count, 2 * model_width).astype(
        jnp.bfloat16
    )
    grad_cross_query = jnp.dot(hidden1_low.T, grad_cross_flat, preferred_element_type=jnp.float32)
    grad_cross_memory = jnp.dot(memory_flat.T, grad_memory_low, preferred_element_type=jnp.float32)
    memory_grad = jnp.dot(
        grad_memory_low, cross_memory.T, preferred_element_type=jnp.float32
    ).reshape(mem_len, row_count, model_width)
    grad_hidden1 = grad_total2 * residual_scale[1] + jnp.dot(
        grad_cross_flat, cross_query.T, preferred_element_type=jnp.float32
    )
    grad_total1, gain_first, shift_first = norm_backward(
        grad_hidden1, normed1, inverse1, norm_gain[0]
    )
    scale_first = jnp.sum(grad_total1 * xfloat, 0)
    grad_first = grad_total1.astype(jnp.bfloat16)
    grad_self_output = jnp.dot(self_attended.T, grad_first, preferred_element_type=jnp.float32)
    grad_self = jnp.dot(grad_first, self_output.T, preferred_element_type=jnp.float32).astype(
        jnp.bfloat16
    )
    grad_self_block = grad_self.reshape(seq_len, row_count, model_width)
    grad_self_heads = to_heads(grad_self_block, head_count)
    self_delta = jnp.sum(grad_self_heads.astype(jnp.float32) * self_heads, -1)
    self_query_step = query_stepper(
        queries, grad_self_heads, self_lse, self_delta, self_key_mask, model_width, head_count
    )
    whole_keys, whole_segs, whole_pads = (
        lax.all_gather(key_values, "seq", axis=0, tiled=True),
        lax.all_gather(seg_columns, "seq", axis=0, tiled=True),
        lax.all_gather(pad_columns, "seq", axis=0, tiled=True),
    )
    grad_queries = block_scan(zero_grid, (whole_keys, whole_segs, whole_pads), 0, self_query_step)
    self_key_step = key_stepper(
        queries, grad_self_heads, self_lse, self_delta, self_key_mask, model_width, head_count
    )
    portion = (whole_keys, whole_segs, whole_pads)
    grad_key_values = lax.psum_scatter(
        block_map(portion, self_key_step).astype(jnp.bfloat16),
        "seq",
        scatter_dimension=0,
        tiled=True,
    ).astype(jnp.float32)
    grad_projected = jnp.concatenate(
        [from_heads(grad_queries), grad_key_values.reshape(token_count, 2 * model_width)], -1
    ).astype(jnp.bfloat16)
    grad_self_project = jnp.dot(flattened.T, grad_projected, preferred_element_type=jnp.float32)
    tokens_grad = (
        grad_total1 * residual_scale[0]
        + jnp.dot(grad_projected, self_project.T, preferred_element_type=jnp.float32)
    ).reshape(seq_len, row_count, model_width)
    norm_pack = jnp.stack(
        [
            gain_first,
            gain_second,
            gain_third,
            shift_first,
            shift_second,
            shift_third,
            scale_first,
            scale_second,
            scale_third,
        ],
        1,
    )
    (
        rows_project,
        rows_output,
        rows_query,
        rows_memory,
        rows_cross_out,
        rows_feed_in,
        rows_in_bias,
        rows_feed_out,
        rows_out_bias,
        rows_pack,
    ) = (
        lax.psum(grad_self_project.astype(jnp.bfloat16), "rows").astype(jnp.float32),
        lax.psum(grad_self_output.astype(jnp.bfloat16), "rows").astype(jnp.float32),
        lax.psum(grad_cross_query.astype(jnp.bfloat16), "rows").astype(jnp.float32),
        lax.psum(grad_cross_memory.astype(jnp.bfloat16), "rows").astype(jnp.float32),
        lax.psum(grad_cross_output.astype(jnp.bfloat16), "rows").astype(jnp.float32),
        lax.psum(grad_feed_in.astype(jnp.bfloat16), "rows").astype(jnp.float32),
        lax.psum(grad_feed_in_bias.astype(jnp.bfloat16), "rows").astype(jnp.float32),
        lax.psum(grad_feed_out.astype(jnp.bfloat16), "rows").astype(jnp.float32),
        lax.psum(grad_feed_out_bias.astype(jnp.bfloat16), "rows").astype(jnp.float32),
        lax.psum(norm_pack.astype(jnp.bfloat16), "rows").astype(jnp.float32),
    )
    (
        share_project,
        share_output,
        share_query,
        share_memory,
        share_cross_out,
        share_feed_in,
        share_in_bias,
        share_feed_out,
        share_out_bias,
        share_pack,
    ) = (
        lax.psum_scatter(
            rows_project.astype(jnp.bfloat16), "seq", scatter_dimension=0, tiled=True
        ).astype(jnp.float32),
        lax.psum_scatter(
            rows_output.astype(jnp.bfloat16), "seq", scatter_dimension=0, tiled=True
        ).astype(jnp.float32),
        lax.psum_scatter(
            rows_query.astype(jnp.bfloat16), "seq", scatter_dimension=0, tiled=True
        ).astype(jnp.float32),
        lax.psum_scatter(
            rows_memory.astype(jnp.bfloat16), "seq", scatter_dimension=0, tiled=True
        ).astype(jnp.float32),
        lax.psum_scatter(
            rows_cross_out.astype(jnp.bfloat16), "seq", scatter_dimension=0, tiled=True
        ).astype(jnp.float32),
        lax.psum_scatter(
            rows_feed_in.astype(jnp.bfloat16), "seq", scatter_dimension=0, tiled=True
        ).astype(jnp.float32),
        lax.psum_scatter(
            rows_in_bias.astype(jnp.bfloat16), "seq", scatter_dimension=0, tiled=True
        ).astype(jnp.float32),
        lax.psum_scatter(
            rows_feed_out.astype(jnp.bfloat16), "seq", scatter_dimension=0, tiled=True
        ).astype(jnp.float32),
        lax.psum_scatter(
            rows_out_bias.astype(jnp.bfloat16), "seq", scatter_dimension=0, tiled=True
        ).astype(jnp.float32),
        lax.psum_scatter(
            rows_pack.astype(jnp.bfloat16), "seq", scatter_dimension=0, tiled=True
        ).astype(jnp.float32),
    )
    return (
        output,
        tokens_grad,
        memory_grad,
        share_project,
        share_output,
        share_query,
        share_memory,
        share_cross_out,
        share_feed_in,
        share_in_bias,
        share_feed_out,
        share_out_bias,
        share_pack[:, 0:3].T,
        share_pack[:, 3:6].T,
        share_pack[:, 6:9].T,
    )


def solution(mesh):
    in_specs = (
        P("seq", "rows", None),
        P("seq", "rows", None),
        P("rows", "seq"),
        P("rows", "seq"),
        P("seq", "rows", None),
        P(),
        P(),
        P(),
        P(),
        P(),
        P(),
        P(),
        P(),
        P(),
        P(),
        P(),
        P(),
    )
    out_specs = (
        P("seq", "rows", None),
        P("seq", "rows", None),
        P("seq", "rows", None),
        P("seq", None),
        P("seq", None),
        P("seq", None),
        P("seq", None),
        P("seq", None),
        P("seq", None),
        P("seq"),
        P("seq", None),
        P("seq"),
        P(None, "seq"),
        P(None, "seq"),
        P(None, "seq"),
    )
    return jax.shard_map(
        on_device, mesh=mesh, in_specs=in_specs, out_specs=out_specs, check_vma=False
    )
```

profile of v0, /device:TPU:0, one launch (start us, length us, event | category | flops | bytes accessed | tf_op | source)
XLA Modules:
  0.0 1029.2 jit_solution(17266654835471261328)
XLA Ops:
  20.0 23.1 %all-gather = s32[16,64,2]{1,2,0:T(2,128)S(1)} all-gather(s32[1,64,2]{1,2,0:T(2,128)S(1)} %bitcast.491), channel_id=1, replica_groups=mesh['seq'=16,'rows'=2] {'seq'}, dimensions={0}, use_global_device_ids=true | all-gather | bytes 8704 | tf_op jit(solution)/shard_map/all_gather | solution.py:357
  46.3 17.9 %all_gather.21 = s32[2048,2]{0,1:T(2,128)S(1)} all-gather(s32[128,2]{0,1:T(2,128)} %bitcast.494), channel_id=1, replica_groups=mesh['seq'=16,'rows'=2] {'seq'}, dimensions={0}, use_global_device_ids=true | all-gather | bytes 17408 | tf_op jit(solution)/shard_map/all_gather | solution.py:329
  64.1 19.3 %all_gather.20 = s32[2048,2]{0,1:T(2,128)S(1)} all-gather(s32[128,2]{0,1:T(2,128)S(1)} %bitcast.462), channel_id=1, replica_groups=mesh['seq'=16,'rows'=2] {'seq'}, dimensions={0}, use_global_device_ids=true | all-gather | bytes 17408 | tf_op jit(solution)/shard_map/all_gather | solution.py:328
  86.2 6.3 copy.131
  92.5 47.6 %all-gather.4.cloned.1.call-done = bf16[2048,2,1024]{2,0,1:T(8,128)(2,1)} async-done(((bf16[128,2,1024]{2,0,1:T(8,128)(2,1)}), bf16[2048,2,1024]{2,0,1:T(8,128)(2,1)}) %all-gather.4.cloned.1.call-update) | async-done | bytes 8388624 | tf_op jit(solution)/shard_map/all_gather | solution.py:327
  140.0 11.5 %copy.124 = bf16[4,512,2,1024]{1,3,2,0:T(8,128)(2,1)} copy(bf16[4,512,2,1024]{3,1,0,2:T(8,128)(2,1)} %bitcast.455) | data formatting | bytes 16777216
  151.6 37.9 %while.153 = (s32[]{:T(128)}, f32[2,8,128]{2,1,0:T(8,128)S(1)}, f32[2,8,128]{2,1,0:T(8,128)S(1)}, f32[2,8,128,64]{2,3,1,0:T(8,128)S(1)}, s32[2,128]{1,0:T(2,128)...) while((s32[]{:T(128)}, f32[2,8,128]{2,1,0:T(8,128)S(1)}, ...), condition=%wide.region_8.9_spmd.clone, body=%wide.region_0.8_spmd.clone.sunk | while | flops 141890176 | bytes 22472236 | solution.py:157
  156.5 9.6 while.161
  157.9 3.3 conditional.18
  162.7 3.3 conditional.18
  170.9 3.0 while.161
  178.7 3.0 while.161
  186.6 3.0 while.161
  199.3 22.7 %while.147 = (s32[]{:T(128)}, f32[2,8,128]{2,1,0:T(8,128)S(1)}, f32[2,8,128]{2,1,0:T(8,128)S(1)}, f32[2,8,128,64]{2,3,1,0:T(8,128)S(1)}, s32[2,128]{1,0:T(2,128)...) while((s32[]{:T(128)}, f32[2,8,128]{2,1,0:T(8,128)S(1)}, ...), condition=%wide.region_19.20_spmd, body=%wide.region_11.19_spmd.sunk | while | flops 141364224 | bytes 22198760 | solution.py:157
  202.7 9.5 while.158
  204.1 3.3 conditional.21
  208.9 3.3 conditional.21
  215.6 6.3 while.158
  218.5 3.3 conditional.21
  238.5 25.0 %while.149 = (s32[]{:T(128)}, f32[2,8,128,64]{2,3,1,0:T(8,128)S(1)}, s32[2,128]{1,0:T(2,128)S(1)}, s32[2,512,2]{1,2,0:T(2,128)S(1)}, bf16[2,512,2,1024]{1,3,2,0:...) while((s32[]{:T(128)}, f32[2,8,128,64]{2,3,1,0:T(8,128)S(1)}, ...), condition=%wide.region_35.36_spmd, body=%wide.region_29.35_spmd.sunk | while | flops 205324288 | bytes 16359344 | solution.py:157
  241.9 10.9 %while.159 = (s32[]{:T(128)}, f32[2,8,128,64]{2,3,1,0:T(8,128)S(1)}, pred[2,128,512]{2,1,0:T(8,128)(4,1)S(1)}, bf16[2,8,128,64]{2,3,1,0:T(8,128)(2,1)S(1)}, bf16...) while((s32[]{:T(128)}, f32[2,8,128,64]{2,3,1,0:T(8,128)S(1)}, ...), condition=%wide.region_34.34_spmd.clone, body=%wide.region_30.33_spmd.clone.sunk | while | flops 205193216 | bytes 7826131 | solution.py:57
  243.3 4.0 conditional.20
  248.8 4.0 conditional.20
  256.3 6.9 while.159
  259.2 4.0 conditional.20
  270.9 42.2 %while.151 = (s32[]{:T(128)}, bf16[2,512,2,1024]{3,1,0,2:T(8,128)(2,1)}, s32[2,128]{1,0:T(2,128)S(1)}, s32[2,512,2]{1,2,0:T(2,128)S(1)}, bf16[2,512,2,1024]{1,3,...) while((s32[]{:T(128)}, ...), condition=%wide.region_60.61_spmd, body=%wide.region_54.60_spmd.sunk | while | flops 275447808 | bytes 37594132 | solution.py:171
  274.3 16.0 %while.160 = (s32[]{:T(128)}, bf16[2,512,1024]{1,2,0:T(8,128)(2,1)}, pred[2,128,512]{2,1,0:T(8,128)(4,1)S(1)}, bf16[2,8,128,64]{2,3,1,0:T(8,128)(2,1)S(1)}, bf16...) while((s32[]{:T(128)}, bf16[2,512,1024]{1,2,0:T(8,128)(2,1)}, ...), condition=%wide.region_59.59_spmd, body=%wide.region_55.58_spmd.sunk | while | flops 275316736 | bytes 20672308 | solution.py:57
  275.6 5.6 conditional.19
  283.5 5.6 conditional.19
  290.3 3.0 copy.198
  298.2 10.5 %while.160 = (s32[]{:T(128)}, bf16[2,512,1024]{1,2,0:T(8,128)(2,1)}, pred[2,128,512]{2,1,0:T(8,128)(4,1)S(1)}, bf16[2,8,128,64]{2,3,1,0:T(8,128)(2,1)S(1)}, bf16...) while((s32[]{:T(128)}, bf16[2,512,1024]{1,2,0:T(8,128)(2,1)}, ...), condition=%wide.region_59.59_spmd, body=%wide.region_55.58_spmd.sunk | while | flops 275316736 | bytes 20672308 | solution.py:57
  301.8 5.6 conditional.19
  308.6 3.0 copy.198
  320.3 68.9 %while.157 = (s32[]{:T(128)}, bf16[4,512,2,1024]{3,1,0,2:T(8,128)(2,1)}, s32[2,128]{1,0:T(2,128)S(1)}, s32[4,512,2]{1,2,0:T(2,128)S(1)}, s32[4]{0:T(128)S(1)}, /...) while((s32[]{:T(128)}, ...), condition=%wide.region_52.53_spmd.clone, body=%wide.region_46.52_spmd.clone.sunk | while | flops 275973760 | bytes 37867616 | solution.py:171
  325.2 16.2 %while.163 = (s32[]{:T(128)}, bf16[2,512,1024]{1,2,0:T(8,128)(2,1)}, pred[2,128,512]{2,1,0:T(8,128)(4,1)S(1)}, bf16[2,8,128,64]{2,3,1,0:T(8,128)(2,1)S(1)}, bf16...) while((s32[]{:T(128)}, bf16[2,512,1024]{1,2,0:T(8,128)(2,1)}, ...), condition=%wide.region_51.51_spmd, body=%wide.region_47.50_spmd.sunk | while | flops 275316736 | bytes 20672308 | solution.py:57
  326.5 5.7 conditional.16
  334.6 5.7 conditional.16
  341.4 3.0 copy.199
  350.7 5.1 while.163
  355.8 3.0 copy.199
  365.1 5.1 while.163
  370.2 3.0 copy.199
  379.6 5.1 while.163
  384.6 3.0 copy.199
  391.8 58.7 %all-reduce.2 = (bf16[2048]{0:T(1024)(128)(2,1)S(1)}, bf16[512]{0:T(512)(128)(2,1)S(1)}) all-reduce(bf16[2048]{0:T(1024)(128)(2,1)S(1)} %copy-done.78, bf16[512]{0:T(512)(128)(2,1)S(1)} %copy-done.80), channel_id=10, replica_groups=mesh['seq'=16,'rows'=2] {'seq'}, use_global_device_ids=true, to_apply=%region_76.77.clone | all-reduce | flops 2560 | bytes 10240
  453.1 3.0 reduce-scatter.23.cloned.1.call-done
  456.1 58.2 %reduce-scatter.21.cloned.1.call-done = bf16[32,512]{1,0:T(8,128)(2,1)} async-done(((bf16[512,512]{1,0:T(8,128)(2,1)}), bf16[32,512]{1,0:T(8,128)(2,1)}) %reduce-scatter.21.cloned.1.call-update) | async-done | bytes 32784 | tf_op jit(solution)/shard_map/reduce_scatter | solution.py:538
  514.4 75.7 %reduce-scatter.19.cloned.1.call-done = bf16[64,2,1024]{2,0,1:T(8,128)(2,1)} async-done(((bf16[1024,2,1024]{2,0,1:T(8,128)(2,1)}), bf16[64,2,1024]{2,0,1:T(8,128)(2,1)}) %reduce-scatter.19.cloned.1.call-update) | async-done | bytes 262160 | tf_op jit(solution)/shard_map/reduce_scatter | solution.py:429
  592.9 49.9 %while.155 = (s32[]{:T(128)}, f32[2,8,128,64]{2,3,1,0:T(8,128)S(1)}, s32[2,128]{1,0:T(2,128)S(1)}, s32[4,512,2]{1,2,0:T(2,128)S(1)}, s32[4]{0:T(128)S(1)}, /*ind...) while((s32[]{:T(128)}, f32[2,8,128,64]{2,3,1,0:T(8,128)S(1)}, ...), condition=%wide.region_45.46_spmd.clone, body=%wide.region_39.45_spmd.clone.sunk | while | flops 205850240 | bytes 16632828 | solution.py:157
  598.8 12.9 %while.162 = (s32[]{:T(128)}, f32[2,8,128,64]{2,3,1,0:T(8,128)S(1)}, pred[2,128,512]{2,1,0:T(8,128)(4,1)}, bf16[2,8,128,64]{2,3,1,0:T(8,128)(2,1)S(1)}, bf16[2,5...) while((s32[]{:T(128)}, f32[2,8,128,64]{2,3,1,0:T(8,128)S(1)}, ...), condition=%wide.region_44.44_spmd.clone, body=%wide.region_40.43_spmd.clone.sunk | while | flops 205193216 | bytes 7826131 | solution.py:57
  601.0 4.1 conditional.17
  607.5 4.2 conditional.17
  617.4 4.6 while.162
  628.0 4.6 while.162
  638.3 4.6 while.162
  643.7 54.1 %reduce-scatter.17.cloned.1.call-done = bf16[128,2,1024]{2,0,1:T(8,128)(2,1)} async-done(((bf16[2048,2,1024]{2,0,1:T(8,128)(2,1)}), bf16[128,2,1024]{2,0,1:T(8,128)(2,1)}) %reduce-scatter.17.cloned.1.call-update) | async-done | bytes 524304 | tf_op jit(solution)/shard_map/reduce_scatter | solution.py:472
  702.0 4.0 convolution_convert_fusion
  710.5 12.8 %all-reduce.8.cloned.1.call-done = (bf16[32,512]{1,0:T(8,128)(2,1)}, bf16[32,512]{1,0:T(8,128)(2,1)}, bf16[32,512]{1,0:T(8,128)(2,1)}, bf16[128]{0:T(256)(128)(2...) async-done(((bf16[32,512]{1,0:T(8,128)(2,1)}, bf16[32,512]{1,0:T(8,128)(2,1)}, bf16[32,512]{1,0:T(8,128)(2,1)}, bf16[128]{0:T(256)(128)(2,1)}, bf16[32]{0:T(256)(128)(2,1)}, ...) | async-done | bytes 99216 | tf_op jit(solution)/shard_map/psum | solution.py:513
  731.0 53.4 %reduce-scatter.33.cloned.1.call-done = bf16[32,1024]{1,0:T(8,128)(2,1)} async-done(((bf16[512,1024]{1,0:T(8,128)(2,1)}), bf16[32,1024]{1,0:T(8,128)(2,1)}) %reduce-scatter.33.cloned.1.call-update) | async-done | bytes 65552
  786.1 60.9 %reduce-scatter.31.cloned.1.call-done = bf16[32,1536]{1,0:T(8,128)(2,1)} async-done(((bf16[512,1536]{1,0:T(8,128)(2,1)}), bf16[32,1536]{1,0:T(8,128)(2,1)}) %reduce-scatter.31.cloned.1.call-update) | async-done | bytes 98320
  848.8 62.4 %reduce-scatter.29.cloned.1.call-done = bf16[128,512]{1,0:T(8,128)(2,1)} async-done(((bf16[2048,512]{1,0:T(8,128)(2,1)}), bf16[128,512]{1,0:T(8,128)(2,1)}) %reduce-scatter.29.cloned.1.call-update) | async-done | bytes 131088 | tf_op jit(solution)/shard_map/reduce_scatter | solution.py:556
  911.2 64.8 %reduce-scatter.27.cloned.1.call-done = bf16[32,2048]{1,0:T(8,128)(2,1)} async-done(((bf16[512,2048]{1,0:T(8,128)(2,1)}), bf16[32,2048]{1,0:T(8,128)(2,1)}) %reduce-scatter.27.cloned.1.call-update) | async-done | bytes 131088 | tf_op jit(solution)/shard_map/reduce_scatter | solution.py:550
  977.4 3.0 convolution_add_fusion.3
  982.5 33.1 %all-reduce.10.cloned.1.call-done = (bf16[32,1536]{0,1:T(8,128)(2,1)}, bf16[32,1024]{0,1:T(8,128)(2,1)}, bf16[32,2048]{1,0:T(8,128)(2,1)}, bf16[128,512]{1,0:T(8,128)(2,1)}) async-done(((bf16[32,1536]{0,1:T(8,128)(2,1)}, bf16[32,1024]{0,1:T(8,128)(2,1)}, bf16[32,2048]{1,0:T(8,128)(2,1)}, bf16[128,512]{1,0:T(8,128)(2,1)}), (bf16[32,1536]{0,1:T(8,128)(2,1)}, bf16[32,1024]{0,1:T(8,128)(2,1)}, ...) | async-done | bytes 426000 | tf_op jit(solution)/shard_map/psum | solution.py:512
  (765 shorter events, 290.7 us)
Async XLA Ops:
  7.2 221.3 %copy-start = (bf16[2048,512]{1,0:T(8,128)(2,1)S(1)}, bf16[2048,512]{1,0:T(8,128)(2,1)}, u32[]{:S(2)}) copy-start(bf16[2048,512]{1,0:T(8,128)(2,1)} %param.65) | copy-start | bytes 6291460
  7.2 3.7 copy-start.60
  7.2 79.0 %all-gather.6.cloned.1.call-start = ((), (), s32[]{:S(2)}) async-start(), calls=%async_computation.11 | async-start | bytes 4456448 | tf_op jit(solution)/shard_map/all_gather | solution.py:356
  10.8 129.2 %all-gather.4.cloned.1.call-start = ((), (), s32[]{:S(2)}) async-start(), calls=%async_computation.10 | async-start | bytes 8912896 | tf_op jit(solution)/shard_map/all_gather | solution.py:327
  11.0 5.1 copy-start.23
  13.1 5.0 copy-start.33
  14.0 5.9 copy-start.47
  14.0 29.3 %copy-start.77 = (f32[3,512]{1,0:T(4,128)S(1)}, f32[3,512]{1,0:T(4,128)}, u32[]{:S(2)}) copy-start(f32[3,512]{1,0:T(4,128)} %param.67) | copy-start | bytes 18436
  18.0 433.7 %reduce-scatter.35.cloned.1.call-start = ((), (), s32[]{:S(2)}) async-start(), calls=%async_computation.21 | async-start | bytes 139264
  157.9 1.8 copy-start.13
  189.6 5.8 copy-start.4
  189.6 5.8 copy-start.24
  189.8 6.9 copy-start.43
  191.6 3.9 copy-start.38
  195.4 3.4 copy-start.34
  195.4 2.0 copy-start.52
  222.0 3.5 copy-start.70
  222.0 3.5 copy-start.74
  222.2 5.1 copy-start.45
  223.6 4.0 copy-start.63
  223.6 4.0 copy-start.67
  223.6 4.0 copy-start.68
  225.5 2.9 copy-start.31
  225.5 2.1 copy-start.35
  227.3 7.9 copy-start.17
  227.3 7.9 copy-start.61
  227.6 7.7 copy-start.65
  228.4 3.2 copy-start.36
  228.5 2.3 copy-start.79
  231.7 2.5 copy-start.53
  263.6 2.8 copy-start.25
  264.7 2.8 copy-start.76
  264.7 3.7 copy-start.32
  268.3 184.8 %reduce-scatter.25.cloned.1.call-start = ((), (), s32[]{:S(2)}) async-start(), calls=%async_computation.16 | async-start | bytes 557056 | tf_op jit(solution)/shard_map/reduce_scatter | solution.py:547
  269.5 186.5 %reduce-scatter.23.cloned.1.call-start = ((), (), s32[]{:S(2)}) async-start(), calls=%async_computation.15 | async-start | bytes 557056 | tf_op jit(solution)/shard_map/reduce_scatter | solution.py:541
  270.9 243.4 %reduce-scatter.21.cloned.1.call-start = ((), (), s32[]{:S(2)}) async-start(), calls=%async_computation.14 | async-start | bytes 557056 | tf_op jit(solution)/shard_map/reduce_scatter | solution.py:538
  275.6 1.9 copy-start.6
  283.6 1.9 copy-start.6
  301.9 1.9 copy-start.6
  313.2 2.4 copy-start.21
  313.2 4.1 copy-start.19
  313.2 4.1 copy-start.44
  315.6 274.5 %reduce-scatter.19.cloned.1.call-start = ((), (), s32[]{:S(2)}) async-start(), calls=%async_computation.13 | async-start | bytes 4456448 | tf_op jit(solution)/shard_map/reduce_scatter | solution.py:429
  317.0 2.3 copy-start.40
  317.0 2.3 copy-start.42
  319.4 378.4 %reduce-scatter.17.cloned.1.call-start = ((), (), s32[]{:S(2)}) async-start(), calls=%async_computation.12 | async-start | bytes 8912896 | tf_op jit(solution)/shard_map/reduce_scatter | solution.py:472
  326.5 1.9 copy-start.7
  334.7 1.9 copy-start.7
  389.2 2.5 copy-start.78
  389.2 2.5 copy-start.80
  389.2 200.8 %copy-start.55 = (bf16[64,2,512]{2,1,0:T(2,128)(2,1)S(1)}, bf16[64,2,512]{2,1,0:T(2,128)(2,1)}, u32[]{:S(2)}) copy-start(bf16[64,2,512]{2,1,0:T(2,128)(2,1)} %param.54) | copy-start | bytes 393220
  389.3 334.1 %all-reduce.8.cloned.1.call-start = ((), (), s32[]{:S(2)}) async-start(), calls=%async_computation.22 | async-start | bytes 206848 | tf_op jit(solution)/shard_map/psum | solution.py:513
  514.3 270.1 %reduce-scatter.33.cloned.1.call-start = ((), (), s32[]{:S(2)}) async-start(), calls=%async_computation.20 | async-start | bytes 1114112
  592.8 254.2 %reduce-scatter.31.cloned.1.call-start = ((), (), s32[]{:S(2)}) async-start(), calls=%async_computation.19 | async-start | bytes 1671168
  643.4 56.3 %copy-start.26 = (bf16[256,512]{1,0:T(8,128)(2,1)S(1)}, bf16[256,512]{1,0:T(8,128)(2,1)}, u32[]{:S(2)}) copy-start(bf16[256,512]{1,0:T(8,128)(2,1)} %copy-done.23) | copy-start | bytes 786436
  701.9 209.3 %reduce-scatter.29.cloned.1.call-start = ((), (), s32[]{:S(2)}) async-start(), calls=%async_computation.18 | async-start | bytes 2228224 | tf_op jit(solution)/shard_map/reduce_scatter | solution.py:556
  706.0 3.6 copy-start.48
  706.0 270.0 %reduce-scatter.27.cloned.1.call-start = ((), (), s32[]{:S(2)}) async-start(), calls=%async_computation.17 | async-start | bytes 2228224 | tf_op jit(solution)/shard_map/reduce_scatter | solution.py:550
  709.6 266.4 %copy-start.30 = (bf16[512,1024]{1,0:T(8,128)(2,1)S(1)}, bf16[512,1024]{1,0:T(8,128)(2,1)}, u32[]{:S(2)}) copy-start(bf16[512,1024]{1,0:T(8,128)(2,1)} %param.61) | copy-start | bytes 3145732
  709.6 266.4 %copy-start.51 = (bf16[64,2,1024]{2,0,1:T(8,128)(2,1)S(1)}, bf16[64,2,1024]{2,0,1:T(8,128)(2,1)}, u32[]{:S(2)}) copy-start(bf16[64,2,1024]{2,0,1:T(8,128)(2,1)} %reduce-scatter.19.cloned.1.call-done) | copy-start | bytes 786436
  709.6 306.0 %all-reduce.10.cloned.1.call-start = ((), (), s32[]{:S(2)}) async-start(), calls=%async_computation.23 | async-start | bytes 1835008 | tf_op jit(solution)/shard_map/psum | solution.py:512
  710.5 267.0 %copy-start.22 = (f32[256,512]{1,0:T(8,128)S(1)}, f32[256,512]{1,0:T(8,128)}, u32[]{:S(2)}) copy-start(f32[256,512]{1,0:T(8,128)} %get-tuple-element.1972) | copy-start | bytes 1572868
  710.5 267.0 %copy-start.73 = (f32[1,512]{1,0:T(1,128)S(1)}, f32[1,512]{1,0:T(1,128)}, u32[]{:S(2)}) copy-start(f32[1,512]{1,0:T(1,128)} %get-tuple-element.2020) | copy-start | bytes 6148
  977.4 45.0 %copy-start.1 = (bf16[2048,512]{1,0:T(8,128)(2,1)S(1)}, bf16[2048,512]{1,0:T(8,128)(2,1)}, u32[]{:S(2)}) copy-start(bf16[2048,512]{1,0:T(8,128)(2,1)} %param.65) | copy-start | bytes 6291460
  (63 other events, 75.6 us)
Sparse Core Ops, SparseCore 0:
  10.9 53.3 all-gather.5
  66.5 73.4 all-gather.3
  268.5 70.5 reduce-scatter.34
  342.4 54.8 reduce-scatter.24
  401.2 54.8 reduce-scatter.22
  459.5 54.7 reduce-scatter.20
  518.6 71.3 reduce-scatter.18
  594.1 103.6 reduce-scatter.16
  701.6 21.6 all-reduce.7
  726.8 57.5 reduce-scatter.32
  788.5 58.4 reduce-scatter.30
  850.6 60.5 reduce-scatter.28
  915.4 60.5 reduce-scatter.26
  978.9 36.7 all-reduce.9
where the time goes:
time: 1040 us; the launch traced here: 1030 us
  waiting for transfers between devices  526 us (51%)
  local copies, waits for them, and re-layouts  175 us (17%)
  blocking collectives  119 us (11%)
  matrix products  92.8 us (9%)
  other arithmetic  63.9 us (6%)
  loops' own time  34.9 us (3%)
  between operations  16.7 us (2%)
    unnamed x17, waiting for transfers between devices  115 us
    reduce_scatter x1, waiting for transfers between devices, on_device(): lax.psum_scatter(block_map(portion, cross_key_step).astype(jnp.bfloat16),...  75.7 us
    reduce_scatter x1, waiting for transfers between devices, on_device(): lax.psum_scatter(rows_feed_in.astype(jnp.bfloat16), 'seq', scatter_dimens...  64.8 us
    reduce_scatter x1, waiting for transfers between devices, on_device(): lax.psum_scatter(rows_feed_out.astype(jnp.bfloat16), 'seq', scatter_dimen...  62.4 us
    unnamed x1, blocking collectives  58.7 us
    reduce_scatter x1, waiting for transfers between devices, on_device(): lax.psum_scatter(rows_output.astype(jnp.bfloat16), 'seq', scatter_dimensi...  58.2 us
    reduce_scatter x1, waiting for transfers between devices, on_device(): lax.psum_scatter(block_map(portion, self_key_step).astype(jnp.bfloat16),...  54.1 us
    all_gather x1, waiting for transfers between devices, on_device(): lax.all_gather(key_values, 'seq', axis=0, tiled=True)  47.6 us
  transfers between devices with their start and end apart: 14, of which 11 were waited for; matrix products, arithmetic and copies ran while one was open for 20% of the time, Pallas kernels for 0%

commit v1 on v0

v1 whole, which is shorter than its diff:
```python
import functools
import math

import jax
import jax.numpy as jnp
from jax import lax
from jax.experimental import pallas as pl
from jax.experimental.pallas import tpu as pltpu
from jax.sharding import PartitionSpec as P

HEADS = 8
EPSILON = 1e-05
NEGATIVE = -1e30
BF = jnp.bfloat16
F32 = jnp.float32
I32 = jnp.int32
MESH = pl.DeviceIdType.MESH
GELU_A = math.sqrt(2.0 / math.pi)
GELU_B = 0.044715


def nn(a, b):
    return jnp.dot(a, b, preferred_element_type=F32)


def nt(a, b):
    return lax.dot_general(a, b, (((1,), (1,)), ((), ())), preferred_element_type=F32)


def tn(a, b):
    return lax.dot_general(a, b, (((0,), (0,)), ((), ())), preferred_element_type=F32)


def log2(value):
    return int(value).bit_length() - 1


def reverse_static(index, bits):
    return sum(((index >> k) & 1) << (bits - 1 - k) for k in range(bits))


class Sizes:
    def __init__(self, n, rows, t, mt, d, ff):
        self.n, self.rows, self.t, self.mt, self.d, self.ff = n, rows, t, mt, d, ff
        self.bits, self.row_bits = log2(n), log2(rows)
        self.split = n // HEADS
        self.hd = d // HEADS
        self.halo = t // 2
        self.mhalo = mt // 2
        self.sums = {
            "fo": (ff // n, d, True),
            "fi": (d // n, ff, True),
            "co": (d // n, d, True),
            "cq": (d // n, d, True),
            "mk": (mt, 2 * d, False),
            "cm": (d // n, 2 * d, True),
            "so": (d // n, d, True),
            "sp": (d // n, 3 * d, True),
        }

    def scratch(self):
        n, t, mt, d, ff, hd = self.n, self.t, self.mt, self.d, self.ff, self.hd
        v, dma = pltpu.VMEM, pltpu.SemaphoreType.DMA
        steps = self.bits + self.row_bits
        spec = dict(
            w_sp=v((d, 3 * d), BF), w_so=v((d, d), BF), w_cq=v((d, d), BF), w_cm=v((d, 2 * d), BF),
            w_co=v((d, d), BF), w_fi=v((d, ff), BF), w_fo=v((ff, d), BF),
            qkvt=v((HEADS, 3 * hd, t), BF), kv=v((n, 2 * hd, t), BF), qt=v((HEADS, hd, t), BF),
            kts=v((hd, n * t), BF), vts=v((hd, n * t), BF),
            ots=v((HEADS, hd, t), BF), otr=v((HEADS, hd, t), BF),
            of=v((HEADS, t, hd), F32), lse=v((HEADS, t, 1), F32),
            dos=v((HEADS, hd, t), BF), dor=v((HEADS, hd, t), BF),
            dqr=v((HEADS, hd, t), BF),
            dkt=v((hd, n * t), F32), dvt=v((hd, n * t), F32),
            dkvr=v((self.split, HEADS, 2 * hd, t), BF),
            qp=v((t, d), BF), ps=v((t + self.halo, 2 * d), BF), pm=v((2 * mt, 2 * d), BF),
            cp=v((8, t), I32), cn=v((8, t), I32),
            lsep=v((HEADS, t, 1), F32), lsec=v((HEADS, t, 1), F32), lsed=v((HEADS, t, 1), F32),
            op=v((t, d), F32), co32=v((2 * t, d), F32),
            dps=v((t + self.halo, 2 * d), F32), dpm=v((2 * mt, 2 * d), F32),
            hss=v((self.halo, 2 * d), BF), hsr=v((self.halo, 2 * d), BF),
            hms=v((mt, 2 * d), BF), hmr=v((mt, 2 * d), BF),
            ag=v((n, mt, 2 * d), BF),
            att=v((2 * t, d), BF), catt=v((2 * t, d), BF), cqv=v((2 * t, d), BF),
            tmp=v((2 * t, d), F32), n1=v((2 * t, d), F32), n2=v((2 * t, d), F32),
            i1=v((2 * t, 1), F32), i2=v((2 * t, 1), F32),
            h1b=v((2 * t, d), BF), h2b=v((2 * t, d), BF),
            act=v((2 * t, ff), BF), dg=v((2 * t, ff), F32),
            dtb=v((2 * t, d), BF), dc=v((2 * t, d), BF), dcq=v((2 * t, d), BF),
            dself=v((t, d), BF), dproj=v((2 * t, 3 * d), BF), dmem=v((2 * mt, 2 * d), BF),
            sm=v((16, d), F32), smr=v((steps, 16, d), F32),
        )
        for name, (r, c, over_rows) in self.sums.items():
            if name != "mk":
                spec["a_" + name] = v((n, r, c), BF)
            spec["r_" + name] = v((n - 1 + (self.row_bits if over_rows else 0), r, c), BF)
            spec["ss_" + name] = dma((steps,))
            spec["rs_" + name] = dma((steps,))
        spec.update(
            sms=dma((steps,)), smrs=dma((steps,)),
            wsem=dma((7,)), ags=dma((self.bits,)), agr=dma((self.bits,)),
            hs=dma((8,)), hr=dma((8,)),
            kvs_s=dma((n,)), kvs_r=dma, q_s=dma((HEADS,)), q_r=dma,
            o_s=dma((HEADS,)), o_r=dma, do_s=dma((HEADS,)), do_r=dma,
            dq_s=dma((HEADS,)), dq_r=dma, dkv_s=dma((n,)), dkv_r=dma,
        )
        return spec


class Refs:
    def __init__(self, names, refs):
        for name, ref in zip(names, refs):
            setattr(self, name, ref)


INPUTS = (
    "x", "mem", "cot", "codes", "segcol",
    "h_sp", "h_so", "h_cq", "h_cm", "h_co", "h_fi", "h_fo",
    "fi_b", "fo_b", "gain", "bias", "scale",
)
OUTPUTS = (
    "out", "dx", "dm", "g_sp", "g_so", "g_cq", "g_cm", "g_co", "g_fi", "g_fo", "g_small",
)


def layer_kernel(z, names, *refs):
    g = Refs(names, refs)
    n, t, mt, d, ff, hd, split = z.n, z.t, z.mt, z.d, z.ff, z.hd, z.split
    half = d // HEADS * 2
    pairs = d // half
    softmax_scale = 1.0 / math.sqrt(hd)
    s = lax.axis_index("seq")
    r = lax.axis_index("rows")
    here = lax.rem(s, n)

    def bit_of(index, k):
        return lax.rem(lax.div(index, 2 ** k), 2)

    def seq_partner(k):
        return s + (1 - 2 * bit_of(s, k)) * 2 ** k

    def row_partner(k):
        return r + (1 - 2 * bit_of(r, k)) * 2 ** k

    nxt = lax.rem(s + 1, n)
    prv = lax.rem(s + n - 1, n)
    place = sum(bit_of(s, k) * 2 ** (z.bits - 1 - k) for k in range(z.bits))
    my_head = lax.div(s, split)
    my_part = lax.rem(s, split)
    own_turn = lax.div(s, split)
    own_rest = lax.rem(s, split)
    own_part = own_rest + lax.rem(own_turn, 2) * (split - 1 - 2 * own_rest)

    barrier = pltpu.get_barrier_semaphore()
    for step in range(1, n):
        pl.semaphore_signal(barrier, inc=1, device_id=(lax.rem(s + step, n), r), device_id_type=MESH)
    for k in range(z.row_bits):
        pl.semaphore_signal(barrier, inc=1, device_id=(s, row_partner(k)), device_id_type=MESH)

    weight_names = ("sp", "cm", "so", "cq", "co", "fi", "fo")
    loads = {}
    for j, name in enumerate(weight_names):
        loads[name] = pltpu.make_async_copy(
            getattr(g, "h_" + name), getattr(g, "w_" + name), g.wsem.at[j]
        )
        loads[name].start()

    def remote(src, dst, ssem, rsem, dev):
        return pltpu.make_async_remote_copy(
            src_ref=src, dst_ref=dst, send_sem=ssem, recv_sem=rsem,
            device_id=dev, device_id_type=MESH,
        )

    class Spread:
        def __init__(self, src, dst, ssem, rsem, dest):
            self.dest = dest
            self.far = remote(src, dst, ssem, rsem, (dest, r))
            self.near = pltpu.make_async_copy(src, dst, rsem)

        def start(self):
            @pl.when(self.dest != s)
            def _():
                self.far.start()

            @pl.when(self.dest == s)
            def _():
                self.near.start()

        def wait_send(self):
            @pl.when(self.dest != s)
            def _():
                self.far.wait_send()

    def wait_whole(ref, sem):
        pltpu.make_async_copy(ref, ref, sem).wait()

    class Sum:
        def __init__(self, name):
            share_rows, columns, over_rows = z.sums[name]
            self.a = g.ag if name == "mk" else getattr(g, "a_" + name)
            self.r = getattr(g, "r_" + name)
            self.ss, self.rs = getattr(g, "ss_" + name), getattr(g, "rs_" + name)
            self.steps = z.bits + (z.row_bits if over_rows else 0)
            self.copies = {}

        def held(self, k):
            if k == 0:
                return self.a, 0, n
            if k <= z.bits:
                first = n - n // 2 ** (k - 1)
                return self.r, first, n // 2 ** k
            return self.r, n - 1 + k - z.bits - 1, 1

        def start(self, k):
            ref, first, blocks = self.held(k)
            into, into_first, into_blocks = self.held(k + 1)
            if k < z.bits:
                count = blocks // 2
                b = bit_of(s, k)
                src = ref.at[pl.ds(first + (1 - b) * count, count)]
                dst = into.at[pl.ds(into_first, count)]
                dev = (seq_partner(k), r)
            else:
                src = ref.at[pl.ds(first, 1)]
                dst = into.at[pl.ds(into_first, 1)]
                dev = (s, row_partner(k - z.bits))
            copy = remote(src, dst, self.ss.at[k], self.rs.at[k], dev)
            copy.start()
            self.copies[k] = copy

        def finish(self, k, out=None):
            self.copies[k].wait()
            ref, first, blocks = self.held(k)
            into, into_first, into_blocks = self.held(k + 1)
            base = first
            if k < z.bits:
                base = first + bit_of(s, k) * (blocks // 2)
            if out is not None:
                out[...] = into[into_first].astype(F32) + ref[base].astype(F32)
                return
            if into_blocks <= 2:
                for j in range(into_blocks):
                    into[into_first + j] = into[into_first + j] + ref[base + j]
            else:
                def add(j, carry):
                    into[into_first + j] = into[into_first + j] + ref[base + j]
                    return carry
                lax.fori_loop(0, into_blocks, add, 0)

        def put(self, owner, value, columns=None):
            where = reverse_static(owner, z.bits)
            if columns is None:
                self.a[where] = value
            else:
                self.a[where, :, columns] = value

    sums = {name: Sum(name) for name in z.sums}

    def put_rows(name, value, columns=None, first_owner=0):
        share = z.sums[name][0]
        value = value.astype(BF)
        for j in range(value.shape[0] // share):
            sums[name].put(first_owner + j, value[j * share:(j + 1) * share], columns)

    def over_rows(count, size, step):
        def one(j, carry):
            step(pl.ds(pl.multiple_of(j * size, size), size))
            return carry
        lax.fori_loop(0, count // size, one, 0)

    def mean(value):
        return jnp.sum(value, -1, keepdims=True) * (1.0 / d)

    def norm_forward(total):
        centred = total - mean(total)
        inverse = lax.rsqrt(mean(centred * centred) + EPSILON)
        return centred * inverse, inverse

    def norm_backward(grad, normed, inverse, gain_row, which):
        scaled = grad * gain_row
        result = inverse * (scaled - mean(scaled) - normed * mean(scaled * normed))
        g.sm[which:which + 1, :] += jnp.sum(grad * normed, 0, keepdims=True)
        g.sm[3 + which:4 + which, :] += jnp.sum(grad, 0, keepdims=True)
        return result

    lane = lax.broadcasted_iota(I32, (t, half), 1)

    def only(value, which):
        keep = (lane < hd) if which == 0 else (lane >= hd)
        return jnp.where(keep, value, jnp.zeros_like(value))

    def both(first, second):
        return jnp.where(lane < hd, first, second)

    def pair_cols(p, offset=0):
        return slice(offset + p * half, offset + (p + 1) * half)

    g.sm[...] = jnp.zeros_like(g.sm)

    loads["sp"].wait()
    for part in range(3):
        cols = slice(part * d, (part + 1) * d)
        doc = nn(g.x[0:t, :], g.w_sp[:, cols]).astype(BF)
        g.qkvt[:, part * hd:(part + 1) * hd, :] = doc.T.reshape(HEADS, hd, t)
    pl.semaphore_wait(barrier, n - 1 + z.row_bits)

    kv_copies = []
    for h in range(HEADS):
        for f in range(split):
            dest = h * split + f
            kv_copies.append(Spread(
                g.qkvt.at[h, pl.ds(hd, 2 * hd)], g.kv.at[here], g.kvs_s.at[dest], g.kvs_r, dest))
    q_copies = [
        Spread(g.qkvt.at[h, pl.ds(0, hd)], g.qt.at[own_turn], g.q_s.at[h], g.q_r, h * split + own_part)
        for h in range(HEADS)
    ]
    for copy in kv_copies + q_copies:
        copy.start()

    packed = nn(g.x[t:, :], g.w_sp[...]).astype(BF)
    g.qp[...] = packed[:, :d]
    g.ps[0:t, :] = packed[:, d:]
    loads["cm"].wait()
    mem_kv = nn(g.mem[...], g.w_cm[...]).astype(BF)
    g.ag[place] = mem_kv[:mt]
    g.pm[z.mhalo:z.mhalo + mt, :] = mem_kv[mt:]

    halo_copies = [
        remote(g.codes, g.cn, g.hs.at[0], g.hr.at[0], (prv, r)),
        remote(g.codes, g.cp, g.hs.at[1], g.hr.at[1], (nxt, r)),
        remote(g.ps.at[pl.ds(t - z.halo, z.halo)], g.ps.at[pl.ds(t, z.halo)],
               g.hs.at[2], g.hr.at[2], (nxt, r)),
        remote(g.pm.at[pl.ds(z.mhalo, z.mhalo)], g.pm.at[pl.ds(z.mhalo + mt, z.mhalo)],
               g.hs.at[3], g.hr.at[3], (prv, r)),
        remote(g.pm.at[pl.ds(mt, z.mhalo)], g.pm.at[pl.ds(0, z.mhalo)],
               g.hs.at[4], g.hr.at[4], (nxt, r)),
    ]
    for copy in halo_copies:
        copy.start()

    class Gather:
        def __init__(self):
            self.copies = {}

        def start(self, k):
            count = 2 ** k
            first = lax.div(place, count) * count
            part = g.ag.at[pl.ds(first, count)]
            self.copies[k] = remote(
                part, part, g.ags.at[k], g.agr.at[k], (seq_partner(z.bits - 1 - k), r))
            self.copies[k].start()

        def finish(self, k):
            self.copies[k].wait()

    gather = Gather()
    gather.start(0)

    for copy in halo_copies[0:3]:
        copy.wait()
    q_at = lax.broadcasted_iota(I32, (t, t), 0)
    k_at = lax.broadcasted_iota(I32, (t, t), 1)
    seg_q = g.segcol[...]

    def self_mask():
        seg_k, pad_k = g.codes[0:1, :], g.codes[1:2, :]
        own = (seg_q == seg_k) & (k_at <= q_at) & ((pad_k == 1) | (k_at == q_at))
        prev = (seg_q == g.cp[2:3, :]) & (g.cp[3:4, :] == 1)
        return own, prev[:, :z.halo]

    def cross_mask():
        at = lax.broadcasted_iota(I32, (1, 2 * mt), 1)
        seg_k = jnp.where(
            at < z.mhalo, g.cp[5:6, :],
            jnp.where(at < z.mhalo + mt, g.codes[4:5, :], g.cn[6:7, :]))
        return seg_q == seg_k

    def softmax_parts(scores):
        top = functools.reduce(jnp.maximum, [jnp.max(b, -1, keepdims=True) for b in scores])
        weights = [jnp.exp(b - top) for b in scores]
        total = functools.reduce(jnp.add, [jnp.sum(w, -1, keepdims=True) for w in weights])
        return weights, total, top + jnp.log(total)

    own_mask, prev_mask = self_mask()
    for p in range(pairs):
        q, k, v = g.qp[:, pair_cols(p)], g.ps[:, pair_cols(p)], g.ps[:, pair_cols(p, d)]
        outs = []
        for w in range(2):
            sc = nt(only(q, w), k) * softmax_scale
            blocks = [jnp.where(own_mask, sc[:, :t], NEGATIVE), jnp.where(prev_mask, sc[:, t:], NEGATIVE)]
            weights, total, lse = softmax_parts(blocks)
            g.lsep[2 * p + w] = lse
            o = nn(weights[0].astype(BF), v[:t]) + nn(weights[1].astype(BF), v[t:])
            outs.append(o / total)
        o = both(*outs)
        g.op[:, pair_cols(p)] = o
        g.att[t:, pair_cols(p)] = o.astype(BF)

    wait_whole(g.kv, g.kvs_r)
    wait_whole(g.qt, g.q_r)
    for j in range(n):
        g.kts[:, j * t:(j + 1) * t] = g.kv[j, 0:hd]
        g.vts[:, j * t:(j + 1) * t] = g.kv[j, hd:]

    wide = split * t
    diag_q = lax.broadcasted_iota(I32, (t, wide), 0)
    diag_k = lax.broadcasted_iota(I32, (t, wide), 1)

    def turn_rest(i):
        return my_part if i % 2 == 0 else split - 1 - my_part

    def diag_mask(i):
        return diag_k <= diag_q + turn_rest(i) * t

    o_copies = []
    for i in range(HEADS):
        q = g.qt[i].T
        low = i * wide
        blocks = []
        if low:
            blocks.append(nn(q, g.kts[:, :low]) * softmax_scale)
        blocks.append(jnp.where(
            diag_mask(i), nn(q, g.kts[:, low:low + wide]) * softmax_scale, NEGATIVE))
        weights, total, lse = softmax_parts(blocks)
        g.lse[i] = lse
        o = nt(weights[-1].astype(BF), g.vts[:, low:low + wide])
        if low:
            o = o + nt(weights[0].astype(BF), g.vts[:, :low])
        o = o / total
        g.of[i] = o
        g.ots[i] = o.T.astype(BF)
        copy = Spread(g.ots.at[i], g.otr.at[my_head], g.o_s.at[i], g.o_r, i * split + turn_rest(i))
        copy.start()
        o_copies.append(copy)
        if i % 2 == 1 and i // 2 < z.bits:
            gather.finish(i // 2)
            if i // 2 + 1 < z.bits:
                gather.start(i // 2 + 1)
    for k in range(HEADS // 2, z.bits):
        gather.finish(k)
        if k + 1 < z.bits:
            gather.start(k + 1)
    for copy in kv_copies + q_copies:
        copy.wait_send()

    loads["so"].wait()
    wait_whole(g.otr, g.o_r)
    g.att[0:t, :] = g.otr[...].reshape(d, t).T
    g.tmp[...] = nn(g.att[...], g.w_so[...])

    def first_norm(rows):
        total = g.x[rows, :].astype(F32) * g.scale[0:1, :] + g.tmp[rows, :]
        normed, inverse = norm_forward(total)
        g.n1[rows, :] = normed
        g.i1[rows, :] = inverse
        g.h1b[rows, :] = (normed * g.gain[0:1, :] + g.bias[0:1, :]).astype(BF)

    over_rows(2 * t, 64, first_norm)
    loads["cq"].wait()
    g.cqv[...] = nn(g.h1b[...], g.w_cq[...]).astype(BF)

    for copy in halo_copies[3:]:
        copy.wait()
    seen = cross_mask()
    for p in range(pairs):
        q, k, v = g.cqv[t:, pair_cols(p)], g.pm[:, pair_cols(p)], g.pm[:, pair_cols(p, d)]
        outs = []
        for w in range(2):
            sc = jnp.where(seen, nt(only(q, w), k) * softmax_scale, NEGATIVE)
            (weights,), total, lse = softmax_parts([sc])
            g.lsec[2 * p + w] = lse
            outs.append(nn(weights.astype(BF), v) / total)
        o = both(*outs)
        g.co32[t:, pair_cols(p)] = o
        g.catt[t:, pair_cols(p)] = o.astype(BF)
    for p in range(pairs):
        q = g.cqv[0:t, pair_cols(p)]
        k = g.ag[:, :, pair_cols(p)].reshape(n * mt, half)
        v = g.ag[:, :, pair_cols(p, d)].reshape(n * mt, half)
        outs = []
        for w in range(2):
            sc = nt(only(q, w), k) * softmax_scale
            (weights,), total, lse = softmax_parts([sc])
            g.lsed[2 * p + w] = lse
            outs.append(nn(weights.astype(BF), v) / total)
        o = both(*outs)
        g.co32[0:t, pair_cols(p)] = o
        g.catt[0:t, pair_cols(p)] = o.astype(BF)
    for copy in o_copies:
        copy.wait_send()

    loads["co"].wait()
    g.tmp[...] = nn(g.catt[...], g.w_co[...])

    def second_norm(rows):
        hidden1 = g.n1[rows, :] * g.gain[0:1, :] + g.bias[0:1, :]
        normed, inverse = norm_forward(hidden1 * g.scale[1:2, :] + g.tmp[rows, :])
        g.n2[rows, :] = normed
        g.i2[rows, :] = inverse
        g.h2b[rows, :] = (normed * g.gain[1:2, :] + g.bias[1:2, :]).astype(BF)

    over_rows(2 * t, 64, second_norm)

    loads["fi"].wait()
    chunks = ff // d
    for c in range(chunks):
        cols = slice(c * d, (c + 1) * d)
        pre = nn(g.h2b[...], g.w_fi[:, cols]) + g.fi_b[0:1, cols]
        square = pre * pre
        bent = jnp.tanh(GELU_A * pre * (1.0 + GELU_B * square))
        g.act[:, cols] = (0.5 * pre * (1.0 + bent)).astype(BF)
        g.dg[:, cols] = 0.5 * (1.0 + bent) + 0.5 * pre * (1.0 - bent * bent) * (
            GELU_A * (1.0 + 3.0 * GELU_B * square))
    loads["fo"].wait()
    g.tmp[...] = nn(g.act[...], g.w_fo[...])

    def third_norm(rows):
        hidden2 = g.n2[rows, :] * g.gain[1:2, :] + g.bias[1:2, :]
        total = hidden2 * g.scale[2:3, :] + (g.tmp[rows, :] + g.fo_b[0:1, :])
        normed, inverse = norm_forward(total)
        g.out[rows, :] = (normed * g.gain[2:3, :] + g.bias[2:3, :]).astype(BF)
        grad = g.cot[rows, :].astype(F32)
        back = norm_backward(grad, normed, inverse, g.gain[2:3, :], 2)
        g.sm[8:9, :] += jnp.sum(back * hidden2, 0, keepdims=True)
        g.dx[rows, :] = back
        low = back.astype(BF)
        g.dtb[rows, :] = low
        g.sm[9:10, :] += jnp.sum(low.astype(F32), 0, keepdims=True)

    over_rows(2 * t, 64, third_norm)

    for c in range(chunks):
        cols = slice(c * d, (c + 1) * d)
        put_rows("fo", nn(g.act[:, cols].T, g.dtb[...]), None, c * d // z.sums["fo"][0])
    sums["fo"].start(0)
    for c in range(chunks):
        cols = slice(c * d, (c + 1) * d)
        back = (nt(g.dtb[...], g.w_fo[cols, :]) * g.dg[:, cols]).astype(BF)
        g.act[:, cols] = back
        g.sm[10 + c:11 + c, :] = jnp.sum(back.astype(F32), 0, keepdims=True)
    sums["fo"].finish(0)
    sums["fo"].start(1)
    h2t = g.h2b[...].T
    for c in range(chunks):
        cols = slice(c * d, (c + 1) * d)
        put_rows("fi", nn(h2t, g.act[:, cols]), cols)
    sums["fi"].start(0)
    g.tmp[...] = nt(g.act[...], g.w_fi[...])

    def second_back(rows):
        grad = g.dx[rows, :] * g.scale[2:3, :] + g.tmp[rows, :]
        back = norm_backward(grad, g.n2[rows, :], g.i2[rows, :], g.gain[1:2, :], 1)
        hidden1 = g.n1[rows, :] * g.gain[0:1, :] + g.bias[0:1, :]
        g.sm[7:8, :] += jnp.sum(back * hidden1, 0, keepdims=True)
        g.dx[rows, :] = back
        g.dtb[rows, :] = back.astype(BF)

    over_rows(2 * t, 64, second_back)
    sums["fo"].finish(1)
    sums["fo"].start(2)
    g.dc[...] = nt(g.dtb[...], g.w_co[...]).astype(BF)
    sums["fi"].finish(0)
    sums["fi"].start(1)

    for p in range(pairs):
        q, k, v = g.cqv[t:, pair_cols(p)], g.pm[:, pair_cols(p)], g.pm[:, pair_cols(p, d)]
        go, o = g.dc[t:, pair_cols(p)], g.co32[t:, pair_cols(p)]
        dqs, dk, dv = [], 0.0, 0.0
        for w in range(2):
            qm, gm = only(q, w), only(go, w)
            weights = jnp.where(seen, jnp.exp(nt(qm, k) * softmax_scale - g.lsec[2 * p + w]), 0.0)
            delta = jnp.sum(gm.astype(F32) * o, -1, keepdims=True)
            ds = (weights * (nt(gm, v) - delta)).astype(BF)
            dqs.append(nn(ds, k))
            dk = dk + tn(ds, qm)
            dv = dv + tn(weights.astype(BF), gm)
        g.dcq[t:, pair_cols(p)] = (both(*dqs) * softmax_scale).astype(BF)
        g.dpm[:, pair_cols(p)] = dk * softmax_scale
        g.dpm[:, pair_cols(p, d)] = dv
    g.hms[0:z.mhalo, :] = g.dpm[0:z.mhalo, :].astype(BF)
    g.hms[z.mhalo:, :] = g.dpm[z.mhalo + mt:, :].astype(BF)
    mem_halo = [
        remote(g.hms.at[pl.ds(0, z.mhalo)], g.hmr.at[pl.ds(z.mhalo, z.mhalo)],
               g.hs.at[5], g.hr.at[5], (prv, r)),
        remote(g.hms.at[pl.ds(z.mhalo, z.mhalo)], g.hmr.at[pl.ds(0, z.mhalo)],
               g.hs.at[6], g.hr.at[6], (nxt, r)),
    ]
    for copy in mem_halo:
        copy.start()
    sums["fo"].finish(2)
    sums["fo"].start(3)

    for p in range(pairs):
        q, go, o = g.cqv[0:t, pair_cols(p)], g.dc[0:t, pair_cols(p)], g.co32[0:t, pair_cols(p)]
        qt, gt = q.T, go.T
        k = g.ag[:, :, pair_cols(p)].reshape(n * mt, half)
        v = g.ag[:, :, pair_cols(p, d)].reshape(n * mt, half)
        dqs, dks, dvs = [], [], []
        for w in range(2):
            qm, gm = only(q, w), only(go, w)
            weights = jnp.exp(nt(qm, k) * softmax_scale - g.lsed[2 * p + w])
            delta = jnp.sum(gm.astype(F32) * o, -1, keepdims=True)
            ds = (weights * (nt(gm, v) - delta)).astype(BF)
            dqs.append(nn(ds, k))
            dks.append(nn(qt[w * hd:(w + 1) * hd], ds))
            dvs.append(nn(gt[w * hd:(w + 1) * hd], weights.astype(BF)))
        g.dcq[0:t, pair_cols(p)] = (both(*dqs) * softmax_scale).astype(BF)
        dk = (jnp.concatenate(dks, 0) * softmax_scale).astype(BF).T
        dv = jnp.concatenate(dvs, 0).astype(BF).T
        g.ag[:, :, pair_cols(p)] = dk.reshape(n, mt, half)
        g.ag[:, :, pair_cols(p, d)] = dv.reshape(n, mt, half)
        if p == 1:
            sums["fi"].finish(1)
            sums["fi"].start(2)
    sums["mk"].start(0)

    put_rows("co", nn(g.catt[...].T, g.dtb[...]))
    put_rows("cq", nn(g.h1b[...].T, g.dcq[...]))
    sums["co"].start(0)
    sums["cq"].start(0)
    g.tmp[...] = nt(g.dcq[...], g.w_cq[...])

    def first_back(rows):
        grad = g.dx[rows, :] * g.scale[1:2, :] + g.tmp[rows, :]
        back = norm_backward(grad, g.n1[rows, :], g.i1[rows, :], g.gain[0:1, :], 0)
        g.sm[6:7, :] += jnp.sum(back * g.x[rows, :].astype(F32), 0, keepdims=True)
        g.dx[rows, :] = back
        g.dtb[rows, :] = back.astype(BF)

    over_rows(2 * t, 64, first_back)
    d_self = nt(g.dtb[...], g.w_so[...]).astype(BF)
    g.dself[...] = d_self[t:]
    g.dos[...] = d_self[:t].T.reshape(HEADS, hd, t)
    do_copies = [
        Spread(g.dos.at[h], g.dor.at[own_turn], g.do_s.at[h], g.do_r, h * split + own_part)
        for h in range(HEADS)
    ]
    for copy in do_copies:
        copy.start()
    put_rows("so", nn(g.att[...].T, g.dtb[...]))
    sums["so"].start(0)
    sums["mk"].finish(0)
    sums["mk"].start(1)
    sums["fo"].finish(3)
    sums["fo"].start(4)
    for name in ("co", "cq"):
        sums[name].finish(0)
        sums[name].start(1)

    for p in range(pairs):
        q, k, v = g.qp[:, pair_cols(p)], g.ps[:, pair_cols(p)], g.ps[:, pair_cols(p, d)]
        go, o = g.dself[:, pair_cols(p)], g.op[:, pair_cols(p)]
        dqs, dk, dv = [], 0.0, 0.0
        for w in range(2):
            qm, gm = only(q, w), only(go, w)
            sc = nt(qm, k) * softmax_scale - g.lsep[2 * p + w]
            weights = jnp.concatenate(
                [jnp.where(own_mask, jnp.exp(sc[:, :t]), 0.0),
                 jnp.where(prev_mask, jnp.exp(sc[:, t:]), 0.0)], 1)
            delta = jnp.sum(gm.astype(F32) * o, -1, keepdims=True)
            ds = (weights * (nt(gm, v) - delta)).astype(BF)
            dqs.append(nn(ds, k))
            dk = dk + tn(ds, qm)
            dv = dv + tn(weights.astype(BF), gm)
        g.dproj[t:, pair_cols(p)] = (both(*dqs) * softmax_scale).astype(BF)
        g.dps[:, pair_cols(p)] = dk * softmax_scale
        g.dps[:, pair_cols(p, d)] = dv
    g.hss[...] = g.dps[t:, :].astype(BF)
    self_halo = remote(g.hss, g.hsr, g.hs.at[7], g.hr.at[7], (prv, r))
    self_halo.start()
    sums["fi"].finish(2)
    sums["fi"].start(3)
    sums["mk"].finish(1)
    sums["mk"].start(2)

    wait_whole(g.dor, g.do_r)
    g.dkt[...] = jnp.zeros_like(g.dkt)
    g.dvt[...] = jnp.zeros_like(g.dvt)
    dq_copies, dkv_copies = [], []
    chunk = min(512, n * t)
    for i in reversed(range(HEADS)):
        qt, gt = g.qt[i], g.dor[i]
        q, go = qt.T, gt.T
        delta = jnp.sum(go.astype(F32) * g.of[i], -1, keepdims=True)
        lse = g.lse[i]
        low = i * wide
        spans = [(a, min(a + chunk, low), False) for a in range(0, low, chunk)]
        spans.append((low, low + wide, True))
        dq = 0.0
        for first, last, masked in spans:
            k, v = g.kts[:, first:last], g.vts[:, first:last]
            weights = jnp.exp(nn(q, k) * softmax_scale - lse)
            if masked:
                weights = jnp.where(diag_mask(i), weights, 0.0)
            ds = (weights * (nn(go, v) - delta)).astype(BF)
            dq = dq + nt(ds, k)
            g.dkt[:, first:last] += nn(qt, ds)
            g.dvt[:, first:last] += nn(gt, weights.astype(BF))
        g.ots[i] = (dq * softmax_scale).T.astype(BF)
        copy = Spread(g.ots.at[i], g.dqr.at[my_head], g.dq_s.at[i], g.dq_r, i * split + turn_rest(i))
        copy.start()
        dq_copies.append(copy)
        for j in range(i * split, (i + 1) * split):
            g.kv[j, 0:hd] = (g.dkt[:, j * t:(j + 1) * t] * softmax_scale).astype(BF)
            g.kv[j, hd:] = g.dvt[:, j * t:(j + 1) * t].astype(BF)
            copy = Spread(g.kv.at[j], g.dkvr.at[my_part, my_head], g.dkv_s.at[j], g.dkv_r, j)
            copy.start()
            dkv_copies.append(copy)
        if i == 6:
            sums["mk"].finish(2)
            sums["mk"].start(3)
        if i == 4:
            sums["fi"].finish(3)
            sums["fi"].start(4)
            for name in ("co", "cq"):
                sums[name].finish(1)
                sums[name].start(2)
            sums["so"].finish(0)
            sums["so"].start(1)
        if i == 2:
            for name in ("co", "cq"):
                sums[name].finish(2)
                sums[name].start(3)
            sums["so"].finish(1)
            sums["so"].start(2)

    for k in range(3, z.bits):
        sums["mk"].finish(k)
        if k + 1 < z.bits:
            sums["mk"].start(k + 1)
    for copy in mem_halo:
        copy.wait()
    ref, first, blocks = sums["mk"].held(z.bits)
    g.dmem[0:mt, :] = ref[first]
    g.dmem[mt:, :] = (g.dpm[z.mhalo:z.mhalo + mt, :] + g.hmr[...].astype(F32)).astype(BF)
    g.dm[...] = nt(g.dmem[...], g.w_cm[...])
    put_rows("cm", nn(g.mem[...].T, g.dmem[...]))
    sums["cm"].start(0)

    self_halo.wait()
    wait_whole(g.dqr, g.dq_r)
    g.dproj[0:t, 0:d] = g.dqr[...].reshape(d, t).T
    wait_whole(g.dkvr, g.dkv_r)
    for part in range(2):
        total = g.dkvr[0, :, part * hd:(part + 1) * hd, :].astype(F32)
        for f in range(1, split):
            total = total + g.dkvr[f, :, part * hd:(part + 1) * hd, :].astype(F32)
        g.dproj[0:t, (part + 1) * d:(part + 2) * d] = total.astype(BF).reshape(d, t).T
    g.dproj[t:2 * t - z.halo, d:] = g.dps[0:t - z.halo, :].astype(BF)
    g.dproj[2 * t - z.halo:, d:] = (g.dps[t - z.halo:t, :] + g.hsr[...].astype(F32)).astype(BF)
    put_rows("sp", nn(g.x[...].T, g.dproj[...]))
    sums["sp"].start(0)

    def small(k):
        dev = (seq_partner(k), r) if k < z.bits else (s, row_partner(k - z.bits))
        return remote(g.sm, g.smr.at[k], g.sms.at[k], g.smrs.at[k], dev)

    g.tmp[...] = nt(g.dproj[...], g.w_sp[...])

    def last(rows):
        g.dx[rows, :] = g.dx[rows, :] * g.scale[0:1, :] + g.tmp[rows, :]

    over_rows(2 * t, 64, last)
    order = ("fo", "fi", "co", "cq", "so", "cm", "sp")
    done = {"fo": 4, "fi": 4, "co": 3, "cq": 3, "so": 2, "cm": 0, "sp": 0}
    for step in range(z.bits + z.row_bits):
        tiny = small(step)
        tiny.start()
        for name in order:
            k = done[name]
            if k >= sums[name].steps:
                continue
            finished = k + 1 == sums[name].steps
            sums[name].finish(k, getattr(g, "g_" + name) if finished else None)
            if not finished:
                sums[name].start(k + 1)
            done[name] = k + 1
        tiny.wait()
        g.sm[...] = g.sm[...] + g.smr[step]
    g.g_small[...] = g.sm[...]
    for copy in do_copies + dq_copies + dkv_copies:
        copy.wait_send()


def on_device(
    mesh_shape,
    tokens, memory, segments, padding, cotangent,
    self_project, self_output, cross_query, cross_memory, cross_output,
    feed_in, feed_in_bias, feed_out, feed_out_bias, norm_gain, norm_bias, residual_scale,
):
    t, _, d = tokens.shape
    mt = memory.shape[0]
    ff = feed_in.shape[1]
    n, rows = mesh_shape
    z = Sizes(n, rows, t, mt, d, ff)

    swap = segments[1, 0] == segments[1, t - 1]

    def ordered(array):
        first, second = array[:, 0], array[:, 1]
        return jnp.concatenate(
            [jnp.where(swap, second, first), jnp.where(swap, first, second)], 0)

    def restored(array):
        first, second = array[:array.shape[0] // 2], array[array.shape[0] // 2:]
        return jnp.stack([jnp.where(swap, second, first), jnp.where(swap, first, second)], 1)

    seg = jnp.where(swap, segments[0], segments[1])
    pad = jnp.where(swap, padding[0], padding[1])
    mem_seg = seg[::2]
    gap = jnp.full((t,), -1, I32)
    tail = jnp.full((t - z.halo,), -1, I32)
    codes = jnp.stack([
        seg, pad,
        jnp.concatenate([seg[t - z.halo:], tail]),
        jnp.concatenate([pad[t - z.halo:], tail]),
        jnp.concatenate([gap[:z.mhalo], mem_seg, gap[:t - z.mhalo - mt]]),
        jnp.concatenate([mem_seg[mt - z.mhalo:], gap[:t - z.mhalo]]),
        jnp.concatenate([gap[:t - z.mhalo], mem_seg[:z.mhalo]]),
        gap,
    ])

    scratch = z.scratch()
    names = INPUTS + OUTPUTS + tuple(scratch)
    vmem, anywhere = pl.BlockSpec(memory_space=pltpu.VMEM), pl.BlockSpec(memory_space=pl.ANY)
    outcome = pl.pallas_call(
        functools.partial(layer_kernel, z, names),
        out_shape=[
            jax.ShapeDtypeStruct((2 * t, d), BF),
            jax.ShapeDtypeStruct((2 * t, d), F32),
            jax.ShapeDtypeStruct((2 * mt, d), F32),
        ] + [
            jax.ShapeDtypeStruct(z.sums[name][:2], F32)
            for name in ("sp", "so", "cq", "cm", "co", "fi", "fo")
        ] + [jax.ShapeDtypeStruct((16, d), F32)],
        in_specs=[vmem] * 5 + [anywhere] * 7 + [vmem] * 5,
        out_specs=[vmem] * len(OUTPUTS),
        scratch_shapes=list(scratch.values()),
        compiler_params=pltpu.CompilerParams(
            collective_id=0, has_side_effects=True, vmem_limit_bytes=62 * 2 ** 20),
        name="layer",
    )(
        ordered(tokens), ordered(memory), ordered(cotangent), codes, seg.reshape(t, 1),
        self_project, self_output, cross_query, cross_memory, cross_output, feed_in, feed_out,
        feed_in_bias.reshape(1, ff), feed_out_bias.reshape(1, d), norm_gain, norm_bias, residual_scale,
    )
    out, dx, dm, g_sp, g_so, g_cq, g_cm, g_co, g_fi, g_fo, small = outcome
    at = lax.axis_index("seq")
    in_bias = lax.dynamic_slice(small[10:10 + ff // d].reshape(ff), (at * (ff // n),), (ff // n,))
    share = lax.dynamic_slice(small, (0, at * (d // n)), (16, d // n))
    return (
        restored(out), restored(dx), restored(dm),
        g_sp, g_so, g_cq, g_cm, g_co, g_fi, in_bias, g_fo, share[9],
        share[0:3], share[3:6], share[6:9],
    )


def solution(mesh):
    in_specs = (
        P("seq", "rows", None), P("seq", "rows", None), P("rows", "seq"), P("rows", "seq"),
        P("seq", "rows", None),
    ) + (P(),) * 12
    out_specs = (P("seq", "rows", None),) * 3 + (
        P("seq", None), P("seq", None), P("seq", None), P("seq", None), P("seq", None),
        P("seq", None), P("seq"), P("seq", None), P("seq"),
        P(None, "seq"), P(None, "seq"), P(None, "seq"),
    )
    shape = (mesh.shape["seq"], mesh.shape["rows"])
    return jax.shard_map(
        functools.partial(on_device, shape),
        mesh=mesh, in_specs=in_specs, out_specs=out_specs, check_vma=False,
    )
```

time: 1040 us -> 215 us (0.21)
  waiting for transfers between devices: 526 us -> 0 us
  Pallas kernels: 0 us -> 187 us
  local copies, waits for them, and re-layouts: 175 us -> 18.1 us
  blocking collectives: 119 us -> 0 us
  matrix products: 92.8 us -> 0 us
  other arithmetic: 63.9 us -> 5.21 us
  loops' own time: 34.9 us -> 0 us
  between operations: 16.7 us -> 2.11 us
    reduce_scatter x7 -> x0, waiting for transfers between devices: 318 us -> none  [the longest x1 75.7 us: on_device(): lax.psum_scatter(block_map(portion, cross_key_step).astype(jnp.bfloat16),...]
    pallas_call x0 -> x1, Pallas kernels: none -> 187 us  [on_device(): pl.pallas_call(functools.partial(layer_kernel, z, names), out_shape=[jax....]
    unnamed x17 -> x0, waiting for transfers between devices: 115 us -> none
    dot_general x56 -> x0, matrix products: 92.8 us -> none  [the longest x15 25.9 us: scores_of(): jnp.einsum('rhqd,krhd->rhqk', queries, key_heads, preferred_element_type=...]
    all_gather x3 -> x0, blocking collectives: 60.3 us -> none  [the longest x1 23.1 us: on_device(): lax.all_gather(memory_columns, 'seq', axis=0, tiled=True)]
    unnamed x1 -> x0, blocking collectives: 58.7 us -> none
    all_gather x2 -> x0, waiting for transfers between devices: 47.6 us -> none  [the longest x1 47.6 us: on_device(): lax.all_gather(key_values, 'seq', axis=0, tiled=True)]
    psum x2 -> x0, waiting for transfers between devices: 46 us -> none  [the longest x1 33.1 us: on_device(): lax.psum(grad_self_project.astype(jnp.bfloat16), 'rows').astype(jnp.float32)]
  transfers between devices with their start and end apart: 14 -> 0, of which waited for: 11 -> 0; matrix products, arithmetic and copies ran while one was open for 20% -> 0% of each run, Pallas kernels for 0% -> 0%
where the time goes in v1:
time: 215 us; the launch traced here: 213 us
  Pallas kernels  187 us (87%)
  local copies, waits for them, and re-layouts  18.1 us (8%)
  other arithmetic  5.21 us (2%)
    pallas_call x1, Pallas kernels, on_device(): pl.pallas_call(functools.partial(layer_kernel, z, names), out_shape=[jax....  187 us
    unnamed x30, local copies, waits for them, and re-layouts  8.47 us

profile of v1, /device:TPU:0, one launch (start us, length us, event | category | flops | bytes accessed | tf_op | source)
XLA Modules:
  0.0 212.7 jit_solution(17892951790639879730)
XLA Ops:
  0.6 1.3 fusion.4
  3.3 0.8 broadcast_select_fusion
  4.0 0.2 slice.106
  4.2 0.1 fusion.5
  4.3 0.1 pad_bitcast_fusion
  4.4 0.1 add_bitcast_fusion
  4.4 0.1 slice_bitcast_fusion.2
  4.5 0.1 slice_bitcast_fusion.1
  4.6 0.6 stack.52.refs_3_
  5.2 1.5 fusion
  6.7 0.0 copy-start
  6.7 1.5 fusion.1
  8.2 0.1 select_bitcast_fusion.7
  8.3 0.7 pad_maximum_fusion.2.refs_2_
  9.0 0.7 pad_maximum_fusion.1.refs_0_
  9.8 0.0 copy-done
  9.8 0.2 fusion.2
  10.0 0.7 pad_maximum_fusion.5.refs_1_
  10.7 0.7 copy.38.refs_4_
  11.4 187.3 %layer.1 = (bf16[256,512]{1,0:T(8,128)(2,1)}, f32[256,512]{1,0:T(8,128)}, f32[128,512]{1,0:T(8,128)}, f32[32,1536]{1,0:T(8,128)}, f32[32,512]{1,0:T(8,128)}, /*i...) custom-call(bf16[256,512]{1,0:T(8,128)(2,1)} %pad_maximum_fusion.1.r, ...), custom_call_target="tpu_custom_call" | custom-call | tf_op jit(solution)/shard_map/layer/pallas_call | solution.py:826
  198.7 1.0 select_bitcast_fusion.3
  199.7 0.0 copy-start.1
  199.7 0.9 copy.41
  200.6 1.1 select_bitcast_fusion.1
  201.7 0.0 copy-start.4
  201.7 0.0 copy-start.8
  201.7 0.0 copy-start.7
  201.7 0.0 copy-start.5
  201.7 0.0 copy-start.6
  201.8 0.0 copy-start.3
  201.8 0.0 copy-start.2
  201.8 1.2 copy.40
  203.0 0.0 copy-done.1
  203.1 1.0 copy.39
  204.0 0.7 slice_bitcast_fusion
  204.8 0.6 dynamic_slice.6
  205.3 1.4 fusion.3
  206.8 1.3 dynamic-slice_bitcast_fusion
  208.0 0.0 copy-done.4
  208.0 0.7 copy.68
  208.7 0.0 copy-done.8
  208.7 0.6 copy.69
  209.4 0.0 copy-done.7
  209.4 0.6 copy.70
  210.0 0.0 copy-done.5
  210.0 0.7 copy.71
  210.6 0.0 copy-done.6
  210.6 0.6 copy.72
  211.3 0.0 copy-done.3
  211.3 0.7 copy.73
  212.0 0.0 copy-done.2
  212.0 0.7 copy.74
  (11 shorter events, 0.2 us)
Async XLA Ops:
  6.7 3.1 %copy-start = (bf16[64,2,512]{2,1,0:T(2,128)(2,1)S(1)}, bf16[64,2,512]{2,1,0:T(2,128)(2,1)}, u32[]{:S(2)}) copy-start(bf16[64,2,512]{2,1,0:T(2,128)(2,1)} %param.18) | copy-start | bytes 393220
  199.7 3.3 %copy-start.1 = (bf16[256,512]{1,0:T(8,128)(2,1)S(1)}, bf16[256,512]{1,0:T(8,128)(2,1)}, u32[]{:S(2)}) copy-start(bf16[256,512]{1,0:T(8,128)(2,1)} %get-tuple-element.26) | copy-start | bytes 786436
  201.7 6.4 %copy-start.4 = (f32[32,1536]{1,0:T(8,128)S(1)}, f32[32,1536]{1,0:T(8,128)}, u32[]{:S(2)}) copy-start(f32[32,1536]{1,0:T(8,128)} %get-tuple-element.99) | copy-start | bytes 589828
  201.7 7.0 %copy-start.8 = (f32[32,512]{1,0:T(8,128)S(1)}, f32[32,512]{1,0:T(8,128)}, u32[]{:S(2)}) copy-start(f32[32,512]{1,0:T(8,128)} %get-tuple-element.100) | copy-start | bytes 196612
  201.7 7.7 %copy-start.7 = (f32[32,512]{1,0:T(8,128)S(1)}, f32[32,512]{1,0:T(8,128)}, u32[]{:S(2)}) copy-start(f32[32,512]{1,0:T(8,128)} %get-tuple-element.101) | copy-start | bytes 196612
  201.7 8.3 %copy-start.5 = (f32[32,1024]{1,0:T(8,128)S(1)}, f32[32,1024]{1,0:T(8,128)}, u32[]{:S(2)}) copy-start(f32[32,1024]{1,0:T(8,128)} %get-tuple-element.102) | copy-start | bytes 393220
  201.7 8.9 %copy-start.6 = (f32[32,512]{1,0:T(8,128)S(1)}, f32[32,512]{1,0:T(8,128)}, u32[]{:S(2)}) copy-start(f32[32,512]{1,0:T(8,128)} %get-tuple-element.103) | copy-start | bytes 196612
  201.8 9.5 %copy-start.3 = (f32[32,2048]{1,0:T(8,128)S(1)}, f32[32,2048]{1,0:T(8,128)}, u32[]{:S(2)}) copy-start(f32[32,2048]{1,0:T(8,128)} %get-tuple-element.104) | copy-start | bytes 786436
  201.8 10.2 %copy-start.2 = (f32[128,512]{1,0:T(8,128)S(1)}, f32[128,512]{1,0:T(8,128)}, u32[]{:S(2)}) copy-start(f32[128,512]{1,0:T(8,128)} %get-tuple-element.106) | copy-start | bytes 786436
